TPU v7x, 256 devices: a whole 4x4x8 slice. The times are simulated.
256 devices in a mesh: tile: 64 (over y, z_hi, x), mem: 4 (over z_lo, core).
Axes of the slice: x: 4, y: 4, z: 8 (z_hi: 4, z_lo: 2; z = z_hi * 2 + z_lo), core: 2. Of those that a mesh axis runs over, the one named last changes fastest.
Arguments:
- perturbations: bfloat16 [32, 16, 512, 256], P('mem', None, 'tile'), may hold values from -6 to 6
- classes: int32 [512, 256], P('tile'), may hold values from 0 to 3
- obs_tile: int32 [65536, 1], P('tile'), may hold values from 0 to 63; in each aligned block of 1024 rows (0 to 1023, 1024 to 2047, ...) at most 48 rows name the same one
- obs_cells: int32 [4, 65536], P(None, 'tile'), may hold values from 0 to 2047
- obs_interp: float32 [4, 65536], P(None, 'tile'), may hold values from 0.1 to 0.6
- obs_jacobian: float32 [16, 65536], P(None, 'tile'), may hold values from 0.1 to 1
- innovation: float32 [65536], P('tile'), may hold values from -10 to 10
- inv_error: float32 [65536], P('tile'), may hold values from 0.5 to 4
Outputs:
- control: float32 [32, 16, 512, 256], P('mem', None, 'tile')
- increment: float32 [16, 512, 256], P('mem', 'tile')
Inputs may be any that keep to these rules, and one draw needn't show every extreme that they name: `obs_tile`: each device's 1024 rows name at most 48 observations in one band; some band gets exactly 48 from some device.
All inputs are finite; a program needn't handle non-finite values.
Results may differ from a plain program's by a relative error of at most 0.0003.
Values sent between devices are 32-bit elements; how exact they have to be, the bound alone decides.
A program may use at most 64 MiB of HBM per device.

v0:
```python
import math

import jax
import jax.numpy as jnp
from jax import lax
from jax.sharding import PartitionSpec as P

SWEEPS = 4


diffusivities = (0.06, 0.1, 0.15, 0.22)
step_length = 0.5


def padded(array, sides, width):
    for axis, dim in sides:
        size, length = (lax.axis_size(axis), array.shape[dim])
        up = [(i, (i + 1) % size) for i in range(size - 1)]
        down = [(j, i) for i, j in up]
        last = lax.slice_in_dim(array, length - width, length, axis=dim)
        initial = lax.slice_in_dim(array, 0, width, axis=dim)
        before = lax.ppermute(last, axis, up)
        after = lax.ppermute(initial, axis, down)
        array = jnp.concatenate([before, array, after], axis=dim)
    return array


def lookup(classes):
    out = jnp.zeros(classes.shape, jnp.float32)
    for position, coefficient in enumerate(diffusivities):
        out = out + jnp.where(classes == position, jnp.float32(coefficient), jnp.float32(0.0))
    return out


def row_mask(rows, margin):
    band = lax.axis_index("tile")
    total_rows = lax.axis_size("tile") * rows
    global_rows = jnp.arange(rows + 2 * margin) + band * rows - margin
    inside = (global_rows >= 0) & (global_rows < total_rows)
    return inside.astype(jnp.float32)


def extend(field, depth):
    rows = field.shape[2]
    wide = padded(field, (("tile", 2),), depth)
    wide = wide * row_mask(rows, depth)[:, None]
    western = wide[..., -depth:]
    eastern = wide[..., :depth]
    return jnp.concatenate([western, wide, eastern], axis=3)


def sweep(grid, coeffs, adjoint):
    source = coeffs * grid if adjoint else grid
    centre = grid[..., 1:-1, 1:-1]
    beside_all = source[..., 2:, 1:-1] + source[..., :-2, 1:-1]
    beside_all = beside_all + source[..., 1:-1, :-2] + source[..., 1:-1, 2:]
    if adjoint:
        return centre + beside_all - 4.0 * source[..., 1:-1, 1:-1]
    return centre + coeffs[..., 1:-1, 1:-1] * (beside_all - 4.0 * centre)


def sweeps(grid, kext, rows, depth, first_index, adjoint):
    grid = sweep(grid, kext, adjoint)
    grid = grid * row_mask(rows, depth - first_index - 1)[:, None]
    return grid


def diffuse(field, kext, adjoint, depth):
    rows = field.shape[2]
    for round_id in range(SWEEPS // depth):
        grid = extend(field, depth)
        field = sweeps(grid, kext, rows, depth, 0, adjoint)
    return field


def on_device(
    perturbations, classes, obs_tile, obs_cells, obs_interp, obs_jacobian, innovation, inv_error
):
    members_local, levels, rows, cols = perturbations.shape
    scale = 1.0 / math.sqrt(members_local * lax.axis_size("mem") - 1)
    tiles = lax.axis_size("tile")
    groups = lax.axis_size("mem")
    share_levels = levels // groups
    depth = 1
    kext = extend(lookup(classes)[None, None], depth)
    cells_tile = rows * cols
    obs_local = obs_tile.shape[0]
    slots = 3 * obs_local // tiles
    target = obs_tile[:, 0]
    onehot = (target[:, None] == jnp.arange(tiles, dtype=jnp.int32)[None, :]).astype(jnp.int32)
    before = jnp.cumsum(onehot, axis=0) - onehot
    rank = jnp.sum(before * onehot, axis=1)
    where_to = target * slots + rank
    payload = jnp.concatenate(
        [
            obs_cells.astype(jnp.float32),
            obs_interp,
            obs_jacobian,
            innovation[None],
            inv_error[None],
        ],
        axis=0,
    )
    width = payload.shape[0]
    buffer = jnp.zeros((width, tiles * slots), jnp.float32).at[:, where_to].set(payload)
    arrived = lax.all_to_all(
        buffer.reshape(width, tiles, slots), "tile", split_axis=1, concat_axis=1, tiled=True
    )
    arrived = arrived.reshape(width, tiles * slots)
    cells = arrived[0:4].astype(jnp.int32)
    weights = arrived[4:8]
    jacobian = arrived[8 : 8 + levels]
    innov = arrived[8 + levels]
    inverse = arrived[9 + levels]

    def adjoint_obs(values, jac):
        contrib = jac * values[None]
        flat = jnp.zeros((jac.shape[0], cells_tile), jnp.float32)
        for c in range(4):
            flat = flat.at[:, cells[c]].add(weights[c] * contrib)
        return flat.reshape(jac.shape[0], rows, cols)

    def member_term(control_now):
        smooth = diffuse(control_now, kext, False, depth)
        return jnp.sum(perturbations * smooth, axis=0)

    def member_adjoint(adjoint_state):
        return diffuse(perturbations * adjoint_state[None] * scale, kext, True, depth)

    def reduced(term):
        return lax.psum(term, "mem") * scale

    start = lax.axis_index("mem") * share_levels
    first = adjoint_obs(-(inverse * innov), jacobian)
    control_one = -step_length * member_adjoint(first)
    state = reduced(member_term(control_one))
    flat = state.reshape(levels, cells_tile)
    mixed = jnp.zeros(jacobian.shape, jnp.float32)
    for c in range(4):
        mixed = mixed + weights[c] * flat[:, cells[c]]
    misfit = inverse * (jnp.sum(jacobian * mixed, axis=0) - innov)
    adjoint_state = adjoint_obs(misfit, jacobian)
    gradient = control_one + member_adjoint(adjoint_state)
    control = control_one - step_length * gradient
    final = reduced(member_term(control))
    final = lax.dynamic_slice_in_dim(final, start, share_levels, 0)
    return (control, final)


def solution(mesh):
    in_specs = (
        P("mem", None, "tile", None),
        P("tile", None),
        P("tile", None),
        P(None, "tile"),
        P(None, "tile"),
        P(None, "tile"),
        P("tile"),
        P("tile"),
    )
    out_specs = (P("mem", None, "tile", None), P("mem", "tile", None))
    return jax.shard_map(
        on_device, mesh=mesh, in_specs=in_specs, out_specs=out_specs, check_vma=False
    )
```

profile of v0, /device:TPU:1, one launch (start us, length us, event | category | flops | bytes accessed | tf_op | source)
XLA Modules:
  0.0 660.5 jit_solution(15899296535733882364)
XLA Ops:
  8.0 18.0 %reduce-window.6 = s32[64,8,128]{2,1,0:T(8,128)S(1)} reduce-window(s32[64,8,128]{2,1,0:T(8,128)S(1)} %fusion.89, s32[]{:T(128)} %constant.26.clone.1), window={size=1x1x128 pad=0_0x0_0x127_0}, to_apply=%region_0.1 | reduce-window | flops 8323072 | bytes 524292 | tf_op jit(solution)/shard_map/reduce-window
  27.0 3.5 scatter_custom_fusion
  32.7 15.1 %all-to-all-start = ((f32[64,1,1248]{2,1,0:T(1,128)}), f32[64,1,1248]{2,1,0:T(1,128)S(1)}, u32[]{:S(2)}, u32[]{:S(2)}) async-start(f32[64,1,1248]{2,1,0:T(1,128)} %reshape.445), calls=%async_computation | async-start | bytes 655360 | tf_op jit(solution)/shard_map/all_to_all | solution.py:106
  49.2 4.0 collective-permute-start.2
  53.9 7.9 %all-to-all-done = f32[64,1,1248]{2,1,0:T(1,128)S(1)} async-done(((f32[64,1,1248]{2,1,0:T(1,128)}), f32[64,1,1248]{2,1,0:T(1,128)S(1)}, u32[]{:S(2)}, u32[]{:S(2)}) %all-to-all-start) | async-done | bytes 319520 | tf_op jit(solution)/shard_map/all_to_all | solution.py:106
  67.6 1.6 copy.176
  70.0 1.6 copy.182
  71.7 1.6 copy.185
  73.4 19.1 %scatter_custom_fusion.1 = f32[16,2048]{0,1:T(8,128)S(1)} fusion(s32[3072]{0:T(1024)} %bitcast.103, f32[3072,16]{1,0:T(8,128)} %copy.176, f32[]{:T(128)} %constant.24.clone.1), kind=kCustom, calls=%fused_computation.181 | custom fusion | flops 49152 | bytes 131584 | tf_op jit(solution)/shard_map/scatter-add | solution.py:120
  92.5 19.1 %scatter_fusion = f32[16,2048]{0,1:T(8,128)S(1)} fusion(f32[16,2048]{0,1:T(8,128)S(1)} %scatter_custom_fusion.1, s32[3072]{0:T(1024)S(1)} %bitcast.90, f32[3072,16]{1,0:T(8,128)S(1)} %copy.179), kind=kCustom, calls=%fused_computation.6 | custom fusion | flops 49152 | bytes 602112 | tf_op jit(solution)/shard_map/scatter-add | solution.py:120
  111.6 19.3 %scatter_fusion.1 = f32[16,2048]{0,1:T(8,128)S(1)} fusion(f32[16,2048]{0,1:T(8,128)S(1)} %scatter_fusion, s32[3072]{0:T(1024)S(1)} %bitcast.93, f32[3072,16]{1,0:T(8,128)} %copy.182), kind=kCustom, calls=%fused_computation.7 | custom fusion | flops 49152 | bytes 602112 | tf_op jit(solution)/shard_map/scatter-add | solution.py:120
  130.9 19.3 %scatter_fusion.2 = f32[16,2048]{0,1:T(8,128)S(1)} fusion(f32[16,2048]{0,1:T(8,128)S(1)} %scatter_fusion.1, s32[3072]{0:T(1024)S(1)} %bitcast.96, f32[3072,16]{1,0:T(8,128)} %copy.185), kind=kCustom, calls=%fused_computation.8 | custom fusion | flops 49152 | bytes 602112 | tf_op jit(solution)/shard_map/scatter-add | solution.py:120
  152.8 6.1 collective-permute-start
  164.6 4.4 collective-permute-start.4
  174.7 4.8 collective-permute-start.6
  184.8 4.4 collective-permute-start.8
  194.9 6.0 collective-permute-start.10
  207.2 7.6 %collective-permute-start.12 = (f32[8,16,1,256]{3,1,2,0:T(8,128)S(1)}, f32[8,16,1,256]{3,1,2,0:T(8,128)S(1)}, u32[]{:S(2)}, u32[]{:S(2)}) collective-permute-start(f32[8,16,1,256]{3,1,2,0:T(8,128)S(1)} %get-tuple-element.82), channel_id=1, source_target_pairs={{0,4},{4,8},{8,12},{12,16},{16,20},{20,24},{24,28},{28,32},{32,36}... | collective-permute-start | bytes 393224 | tf_op jit(solution)/shard_map/ppermute | solution.py:22
  219.3 7.5 %collective-permute-start.14 = (f32[8,16,1,256]{3,1,2,0:T(8,128)S(1)}, f32[8,16,1,256]{3,1,2,0:T(8,128)S(1)}, u32[]{:S(2)}, u32[]{:S(2)}) collective-permute-start(f32[8,16,1,256]{3,1,2,0:T(8,128)S(1)} %get-tuple-element.80), channel_id=1, source_target_pairs={{0,4},{4,8},{8,12},{12,16},{16,20},{20,24},{24,28},{28,32},{32,36}... | collective-permute-start | bytes 393224 | tf_op jit(solution)/shard_map/ppermute | solution.py:22
  231.3 7.5 %collective-permute-start.16 = (f32[8,16,1,256]{3,1,2,0:T(8,128)S(1)}, f32[8,16,1,256]{3,1,2,0:T(8,128)S(1)}, u32[]{:S(2)}, u32[]{:S(2)}) collective-permute-start(f32[8,16,1,256]{3,1,2,0:T(8,128)S(1)} %get-tuple-element.78), channel_id=1, source_target_pairs={{0,4},{4,8},{8,12},{12,16},{16,20},{20,24},{24,28},{28,32},{32,36}... | collective-permute-start | bytes 393224 | tf_op jit(solution)/shard_map/ppermute | solution.py:22
  242.9 83.8 %all-reduce.3.cloned.1.call-done = f32[16,8,256]{2,0,1:T(8,128)} async-done(((f32[16,8,256]{2,0,1:T(8,128)}), f32[16,8,256]{2,0,1:T(8,128)}) %all-reduce.3.cloned.1.call-update) | async-done | bytes 131088 | tf_op jit(solution)/shard_map/psum | solution.py:131
  328.0 10.8 %gather_fusion.3 = f32[3072,16]{1,0:T(8,128)} fusion(f32[16,2048]{0,1:T(8,128)S(1)} %bitcast.73, s32[3072]{0:T(1024)S(1)} %broadcast_clamp_fusion), kind=kCustom, calls=%fused_computation.3 | custom fusion | bytes 405504 | tf_op jit(solution)/shard_map/gather | solution.py:140
  338.8 2.8 copy.195
  341.6 10.8 %gather_fusion.2 = f32[3072,16]{1,0:T(8,128)} fusion(f32[16,2048]{0,1:T(8,128)S(1)} %bitcast.74, s32[3072]{0:T(1024)S(1)} %broadcast_clamp_fusion.1), kind=kCustom, calls=%fused_computation.2 | custom fusion | bytes 405504 | tf_op jit(solution)/shard_map/gather | solution.py:140
  352.4 2.8 copy.193
  355.3 10.8 %gather_fusion.1 = f32[3072,16]{1,0:T(8,128)} fusion(f32[16,2048]{0,1:T(8,128)S(1)} %bitcast.75, s32[3072]{0:T(1024)S(1)} %broadcast_clamp_fusion.2), kind=kCustom, calls=%fused_computation.1 | custom fusion | bytes 405504 | tf_op jit(solution)/shard_map/gather | solution.py:140
  366.1 2.8 copy.191
  368.9 10.8 %gather_fusion = f32[3072,16]{1,0:T(8,128)} fusion(f32[16,2048]{0,1:T(8,128)S(1)} %bitcast.76, s32[3072]{0:T(1024)S(1)} %broadcast_clamp_fusion.3), kind=kCustom, calls=%fused_computation | custom fusion | bytes 405504 | tf_op jit(solution)/shard_map/gather | solution.py:140
  379.7 2.9 copy.189
  384.9 1.6 copy.197
  386.6 19.1 %scatter_custom_fusion.5 = f32[16,2048]{0,1:T(8,128)S(1)} fusion(s32[3072]{0:T(1024)S(1)} %bitcast.105, f32[3072,16]{1,0:T(8,128)} %copy.197, f32[]{:T(128)} %constant.24.clone.1), kind=kCustom, calls=%fused_computation.179 | custom fusion | flops 49152 | bytes 131584 | tf_op jit(solution)/shard_map/scatter-add | solution.py:120
  405.7 1.6 copy.198
  407.4 1.6 copy.199
  409.0 1.6 copy.200
  410.6 19.3 %scatter_fusion.3 = f32[16,2048]{0,1:T(8,128)S(1)} fusion(f32[16,2048]{0,1:T(8,128)S(1)} %scatter_custom_fusion.5, s32[3072]{0:T(1024)S(1)} %bitcast.92, f32[3072,16]{1,0:T(8,128)} %copy.198), kind=kCustom, calls=%fused_computation.10 | custom fusion | flops 49152 | bytes 602112 | tf_op jit(solution)/shard_map/scatter-add | solution.py:120
  429.9 19.3 %scatter_fusion.4 = f32[16,2048]{0,1:T(8,128)S(1)} fusion(f32[16,2048]{0,1:T(8,128)S(1)} %scatter_fusion.3, s32[3072]{0:T(1024)S(1)} %bitcast.95, f32[3072,16]{1,0:T(8,128)} %copy.199), kind=kCustom, calls=%fused_computation.11 | custom fusion | flops 49152 | bytes 602112 | tf_op jit(solution)/shard_map/scatter-add | solution.py:120
  449.2 19.5 %scatter_fusion.5 = f32[16,2048]{0,1:T(8,128)S(1)} fusion(f32[16,2048]{0,1:T(8,128)S(1)} %scatter_fusion.4, s32[3072]{0:T(1024)S(1)} %bitcast.98, f32[3072,16]{1,0:T(8,128)} %copy.200), kind=kCustom, calls=%fused_computation.12 | custom fusion | flops 49152 | bytes 602112 | tf_op jit(solution)/shard_map/scatter-add | solution.py:120
  470.5 6.7 %collective-permute-start.18 = (f32[8,16,1,256]{3,1,2,0:T(8,128)S(1)}, f32[8,16,1,256]{3,1,2,0:T(8,128)S(1)}, u32[]{:S(2)}, u32[]{:S(2)}) collective-permute-start(f32[8,16,1,256]{3,1,2,0:T(8,128)S(1)} %get-tuple-element.66), channel_id=1, source_target_pairs={{0,4},{4,8},{8,12},{12,16},{16,20},{20,24},{24,28},{28,32},{32,36}... | collective-permute-start | bytes 393224 | tf_op jit(solution)/shard_map/ppermute | solution.py:22
  477.2 1.8 collective-permute-done.19
  483.7 4.7 collective-permute-start.20
  494.1 4.4 collective-permute-start.22
  504.2 7.3 %collective-permute-start.24 = (f32[8,16,1,256]{3,1,2,0:T(8,128)S(1)}, f32[8,16,1,256]{3,1,2,0:T(8,128)S(1)}, u32[]{:S(2)}, u32[]{:S(2)}) collective-permute-start(f32[8,16,1,256]{3,1,2,0:T(8,128)S(1)} %get-tuple-element.60), channel_id=1, source_target_pairs={{0,4},{4,8},{8,12},{12,16},{16,20},{20,24},{24,28},{28,32},{32,36}... | collective-permute-start | bytes 393224 | tf_op jit(solution)/shard_map/ppermute | solution.py:22
  517.2 8.6 %collective-permute-start.26 = (f32[8,16,1,256]{3,1,2,0:T(8,128)S(1)}, f32[8,16,1,256]{3,1,2,0:T(8,128)S(1)}, u32[]{:S(2)}, u32[]{:S(2)}) collective-permute-start(f32[8,16,1,256]{3,1,2,0:T(8,128)S(1)} %get-tuple-element.58), channel_id=1, source_target_pairs={{0,4},{4,8},{8,12},{12,16},{16,20},{20,24},{24,28},{28,32},{32,36}... | collective-permute-start | bytes 393224 | tf_op jit(solution)/shard_map/ppermute | solution.py:22
  530.3 8.1 %collective-permute-start.28 = (f32[8,16,1,256]{3,1,2,0:T(8,128)S(1)}, f32[8,16,1,256]{3,1,2,0:T(8,128)S(1)}, u32[]{:S(2)}, u32[]{:S(2)}) collective-permute-start(f32[8,16,1,256]{3,1,2,0:T(8,128)S(1)} %get-tuple-element.56), channel_id=1, source_target_pairs={{0,4},{4,8},{8,12},{12,16},{16,20},{20,24},{24,28},{28,32},{32,36}... | collective-permute-start | bytes 393224 | tf_op jit(solution)/shard_map/ppermute | solution.py:22
  542.9 8.1 %collective-permute-start.30 = (f32[8,16,1,256]{3,1,2,0:T(8,128)S(1)}, f32[8,16,1,256]{3,1,2,0:T(8,128)S(1)}, u32[]{:S(2)}, u32[]{:S(2)}) collective-permute-start(f32[8,16,1,256]{3,1,2,0:T(8,128)S(1)} %get-tuple-element.54), channel_id=1, source_target_pairs={{0,4},{4,8},{8,12},{12,16},{16,20},{20,24},{24,28},{28,32},{32,36}... | collective-permute-start | bytes 393224 | tf_op jit(solution)/shard_map/ppermute | solution.py:22
  551.2 1.8 collective-permute-done.30
  555.5 10.6 %collective-permute-start.32 = (f32[8,16,1,256]{3,1,2,0:T(8,128)S(1)}, f32[8,16,1,256]{3,1,2,0:T(8,128)S(1)}, u32[]{:S(2)}, u32[]{:S(2)}) collective-permute-start(f32[8,16,1,256]{3,1,2,0:T(8,128)S(1)} %get-tuple-element.52), channel_id=1, source_target_pairs={{0,4},{4,8},{8,12},{12,16},{16,20},{20,24},{24,28},{28,32},{32,36}... | collective-permute-start | bytes 393224 | tf_op jit(solution)/shard_map/ppermute | solution.py:22
  571.6 80.2 %all-reduce.5.cloned.1.call-done = f32[16,8,256]{2,0,1:T(8,128)} async-done(((f32[16,8,256]{2,0,1:T(8,128)}), f32[16,8,256]{2,0,1:T(8,128)}) %all-reduce.5.cloned.1.call-update) | async-done | bytes 131088 | tf_op jit(solution)/shard_map/psum | solution.py:131
  (252 shorter events, 101.7 us)
Async XLA Ops:
  7.2 19.4 %copy-start.22 = (s32[1024,1]{0,1:T(1,128)S(1)}, s32[1024,1]{0,1:T(1,128)}, u32[]{:S(2)}) copy-start(s32[1024,1]{0,1:T(1,128)} %param.10) | copy-start | bytes 12292
  7.2 19.5 %copy-start.23 = (s32[4,1024]{1,0:T(4,128)S(1)}, s32[4,1024]{1,0:T(4,128)}, u32[]{:S(2)}) copy-start(s32[4,1024]{1,0:T(4,128)} %param.11) | copy-start | bytes 49156
  7.2 19.5 %copy-start.24 = (f32[4,1024]{1,0:T(4,128)S(1)}, f32[4,1024]{1,0:T(4,128)}, u32[]{:S(2)}) copy-start(f32[4,1024]{1,0:T(4,128)} %param.12) | copy-start | bytes 49156
  7.2 19.5 %copy-start.20 = (f32[16,1024]{1,0:T(8,128)S(1)}, f32[16,1024]{1,0:T(8,128)}, u32[]{:S(2)}) copy-start(f32[16,1024]{1,0:T(8,128)} %param.13) | copy-start | bytes 196612
  7.2 19.5 %copy-start.26 = (f32[1024]{0:T(1024)S(1)}, f32[1024]{0:T(1024)}, u32[]{:S(2)}) copy-start(f32[1024]{0:T(1024)} %param.14) | copy-start | bytes 12292
  7.2 19.5 %copy-start.27 = (f32[1024]{0:T(1024)S(1)}, f32[1024]{0:T(1024)}, u32[]{:S(2)}) copy-start(f32[1024]{0:T(1024)} %param.15) | copy-start | bytes 12292
  31.1 16.7 %copy-start.25 = (s32[8,256]{1,0:T(8,128)S(1)}, s32[8,256]{1,0:T(8,128)}, u32[]{:S(2)}) copy-start(s32[8,256]{1,0:T(8,128)} %param.9) | copy-start | bytes 24580
  32.7 29.2 %all-to-all-start = ((f32[64,1,1248]{2,1,0:T(1,128)}), f32[64,1,1248]{2,1,0:T(1,128)S(1)}, u32[]{:S(2)}, u32[]{:S(2)}) async-start(f32[64,1,1248]{2,1,0:T(1,128)} %reshape.445), calls=%async_computation | async-start | bytes 655360 | tf_op jit(solution)/shard_map/all_to_all | solution.py:106
  47.8 278.9 %all-reduce.3.cloned.1.call-start = ((), (), s32[]{:S(2)}) async-start(), calls=%async_computation.1 | async-start | bytes 262144 | tf_op jit(solution)/shard_map/psum | solution.py:131
  47.9 5.3 collective-permute-start.3
  49.2 4.7 collective-permute-start.2
  151.5 7.8 %collective-permute-start.1 = (f32[8,16,1,256]{3,1,2,0:T(8,128)S(1)}, f32[8,16,1,256]{3,1,2,0:T(8,128)S(1)}, u32[]{:S(2)}, u32[]{:S(2)}) collective-permute-start(f32[8,16,1,256]{3,1,2,0:T(8,128)S(1)} %get-tuple-element.93), channel_id=1, source_target_pairs={{4,0},{8,4},{12,8},{16,12},{20,16},{24,20},{28,24},{32,28},{36,32}... | collective-permute-start | bytes 393224 | tf_op jit(solution)/shard_map/ppermute | solution.py:23
  152.8 8.1 %collective-permute-start = (f32[8,16,1,256]{3,1,2,0:T(8,128)S(1)}, f32[8,16,1,256]{3,1,2,0:T(8,128)S(1)}, u32[]{:S(2)}, u32[]{:S(2)}) collective-permute-start(f32[8,16,1,256]{3,1,2,0:T(8,128)S(1)} %get-tuple-element.92), channel_id=1, source_target_pairs={{0,4},{4,8},{8,12},{12,16},{16,20},{20,24},{24,28},{28,32},{32,36}... | collective-permute-start | bytes 393224 | tf_op jit(solution)/shard_map/ppermute | solution.py:22
  163.3 6.1 collective-permute-start.5
  164.6 6.3 collective-permute-start.4
  173.4 6.1 collective-permute-start.7
  174.7 6.3 collective-permute-start.6
  183.5 6.1 collective-permute-start.9
  184.8 6.3 collective-permute-start.8
  193.6 8.4 %copy-start.5 = (f32[1,64,48]{2,0,1:T(1,128)S(1)}, f32[1,64,48]{2,0,1:T(1,128)}, u32[]{:S(2)}) copy-start(f32[1,64,48]{2,0,1:T(1,128)} %get-tuple-element.77) | copy-start | bytes 36868
  193.6 11.0 %collective-permute-start.11 = (f32[8,16,1,256]{3,1,2,0:T(8,128)S(1)}, f32[8,16,1,256]{3,1,2,0:T(8,128)S(1)}, u32[]{:S(2)}, u32[]{:S(2)}) collective-permute-start(f32[8,16,1,256]{3,1,2,0:T(8,128)S(1)} %get-tuple-element.85), channel_id=1, source_target_pairs={{4,0},{8,4},{12,8},{16,12},{20,16},{24,20},{28,24},{32,28},{36,32}... | collective-permute-start | bytes 393224 | tf_op jit(solution)/shard_map/ppermute | solution.py:23
  194.9 9.7 %collective-permute-start.10 = (f32[8,16,1,256]{3,1,2,0:T(8,128)S(1)}, f32[8,16,1,256]{3,1,2,0:T(8,128)S(1)}, u32[]{:S(2)}, u32[]{:S(2)}) collective-permute-start(f32[8,16,1,256]{3,1,2,0:T(8,128)S(1)} %get-tuple-element.84), channel_id=1, source_target_pairs={{0,4},{4,8},{8,12},{12,16},{16,20},{20,24},{24,28},{28,32},{32,36}... | collective-permute-start | bytes 393224 | tf_op jit(solution)/shard_map/ppermute | solution.py:22
  205.9 9.3 %collective-permute-start.13 = (f32[8,16,1,256]{3,1,2,0:T(8,128)S(1)}, f32[8,16,1,256]{3,1,2,0:T(8,128)S(1)}, u32[]{:S(2)}, u32[]{:S(2)}) collective-permute-start(f32[8,16,1,256]{3,1,2,0:T(8,128)S(1)} %get-tuple-element.83), channel_id=1, source_target_pairs={{4,0},{8,4},{12,8},{16,12},{20,16},{24,20},{28,24},{32,28},{36,32}... | collective-permute-start | bytes 393224 | tf_op jit(solution)/shard_map/ppermute | solution.py:23
  207.2 9.5 %collective-permute-start.12 = (f32[8,16,1,256]{3,1,2,0:T(8,128)S(1)}, f32[8,16,1,256]{3,1,2,0:T(8,128)S(1)}, u32[]{:S(2)}, u32[]{:S(2)}) collective-permute-start(f32[8,16,1,256]{3,1,2,0:T(8,128)S(1)} %get-tuple-element.82), channel_id=1, source_target_pairs={{0,4},{4,8},{8,12},{12,16},{16,20},{20,24},{24,28},{28,32},{32,36}... | collective-permute-start | bytes 393224 | tf_op jit(solution)/shard_map/ppermute | solution.py:22
  218.0 9.2 %collective-permute-start.15 = (f32[8,16,1,256]{3,1,2,0:T(8,128)S(1)}, f32[8,16,1,256]{3,1,2,0:T(8,128)S(1)}, u32[]{:S(2)}, u32[]{:S(2)}) collective-permute-start(f32[8,16,1,256]{3,1,2,0:T(8,128)S(1)} %get-tuple-element.81), channel_id=1, source_target_pairs={{4,0},{8,4},{12,8},{16,12},{20,16},{24,20},{28,24},{32,28},{36,32}... | collective-permute-start | bytes 393224 | tf_op jit(solution)/shard_map/ppermute | solution.py:23
  219.3 9.4 %collective-permute-start.14 = (f32[8,16,1,256]{3,1,2,0:T(8,128)S(1)}, f32[8,16,1,256]{3,1,2,0:T(8,128)S(1)}, u32[]{:S(2)}, u32[]{:S(2)}) collective-permute-start(f32[8,16,1,256]{3,1,2,0:T(8,128)S(1)} %get-tuple-element.80), channel_id=1, source_target_pairs={{0,4},{4,8},{8,12},{12,16},{16,20},{20,24},{24,28},{28,32},{32,36}... | collective-permute-start | bytes 393224 | tf_op jit(solution)/shard_map/ppermute | solution.py:22
  230.0 9.2 %collective-permute-start.17 = (f32[8,16,1,256]{3,1,2,0:T(8,128)S(1)}, f32[8,16,1,256]{3,1,2,0:T(8,128)S(1)}, u32[]{:S(2)}, u32[]{:S(2)}) collective-permute-start(f32[8,16,1,256]{3,1,2,0:T(8,128)S(1)} %get-tuple-element.79), channel_id=1, source_target_pairs={{4,0},{8,4},{12,8},{16,12},{20,16},{24,20},{28,24},{32,28},{36,32}... | collective-permute-start | bytes 393224 | tf_op jit(solution)/shard_map/ppermute | solution.py:23
  231.3 9.4 %collective-permute-start.16 = (f32[8,16,1,256]{3,1,2,0:T(8,128)S(1)}, f32[8,16,1,256]{3,1,2,0:T(8,128)S(1)}, u32[]{:S(2)}, u32[]{:S(2)}) collective-permute-start(f32[8,16,1,256]{3,1,2,0:T(8,128)S(1)} %get-tuple-element.78), channel_id=1, source_target_pairs={{0,4},{4,8},{8,12},{12,16},{16,20},{20,24},{24,28},{28,32},{32,36}... | collective-permute-start | bytes 393224 | tf_op jit(solution)/shard_map/ppermute | solution.py:22
  242.7 409.1 %all-reduce.5.cloned.1.call-start = ((), (), s32[]{:S(2)}) async-start(), calls=%async_computation.2 | async-start | bytes 262144 | tf_op jit(solution)/shard_map/psum | solution.py:131
  379.7 3.0 copy-start.17
  379.7 3.0 copy-start.18
  384.9 20.8 %copy-start.4 = (f32[3072,16]{0,1:T(8,128)S(1)}, f32[3072,16]{0,1:T(8,128)}, u32[]{:S(2)}) copy-start(f32[3072,16]{0,1:T(8,128)} %get-tuple-element.95) | copy-start | bytes 589828
  469.2 9.9 %collective-permute-start.19 = (f32[8,16,1,256]{3,1,2,0:T(8,128)S(1)}, f32[8,16,1,256]{3,1,2,0:T(8,128)S(1)}, u32[]{:S(2)}, u32[]{:S(2)}) collective-permute-start(f32[8,16,1,256]{3,1,2,0:T(8,128)S(1)} %get-tuple-element.67), channel_id=1, source_target_pairs={{4,0},{8,4},{12,8},{16,12},{20,16},{24,20},{28,24},{32,28},{36,32}... | collective-permute-start | bytes 393224 | tf_op jit(solution)/shard_map/ppermute | solution.py:23
  470.5 9.5 %collective-permute-start.18 = (f32[8,16,1,256]{3,1,2,0:T(8,128)S(1)}, f32[8,16,1,256]{3,1,2,0:T(8,128)S(1)}, u32[]{:S(2)}, u32[]{:S(2)}) collective-permute-start(f32[8,16,1,256]{3,1,2,0:T(8,128)S(1)} %get-tuple-element.66), channel_id=1, source_target_pairs={{0,4},{4,8},{8,12},{12,16},{16,20},{20,24},{24,28},{28,32},{32,36}... | collective-permute-start | bytes 393224 | tf_op jit(solution)/shard_map/ppermute | solution.py:22
  482.4 7.0 %collective-permute-start.21 = (f32[8,16,1,256]{3,1,2,0:T(8,128)S(1)}, f32[8,16,1,256]{3,1,2,0:T(8,128)S(1)}, u32[]{:S(2)}, u32[]{:S(2)}) collective-permute-start(f32[8,16,1,256]{3,1,2,0:T(8,128)S(1)} %get-tuple-element.65), channel_id=1, source_target_pairs={{4,0},{8,4},{12,8},{16,12},{20,16},{24,20},{28,24},{32,28},{36,32}... | collective-permute-start | bytes 393224 | tf_op jit(solution)/shard_map/ppermute | solution.py:23
  483.7 6.7 %collective-permute-start.20 = (f32[8,16,1,256]{3,1,2,0:T(8,128)S(1)}, f32[8,16,1,256]{3,1,2,0:T(8,128)S(1)}, u32[]{:S(2)}, u32[]{:S(2)}) collective-permute-start(f32[8,16,1,256]{3,1,2,0:T(8,128)S(1)} %get-tuple-element.64), channel_id=1, source_target_pairs={{0,4},{4,8},{8,12},{12,16},{16,20},{20,24},{24,28},{28,32},{32,36}... | collective-permute-start | bytes 393224 | tf_op jit(solution)/shard_map/ppermute | solution.py:22
  492.8 6.1 collective-permute-start.23
  494.1 6.3 collective-permute-start.22
  502.9 9.0 %collective-permute-start.25 = (f32[8,16,1,256]{3,1,2,0:T(8,128)S(1)}, f32[8,16,1,256]{3,1,2,0:T(8,128)S(1)}, u32[]{:S(2)}, u32[]{:S(2)}) collective-permute-start(f32[8,16,1,256]{3,1,2,0:T(8,128)S(1)} %get-tuple-element.61), channel_id=1, source_target_pairs={{4,0},{8,4},{12,8},{16,12},{20,16},{24,20},{28,24},{32,28},{36,32}... | collective-permute-start | bytes 393224 | tf_op jit(solution)/shard_map/ppermute | solution.py:23
  504.2 9.3 %collective-permute-start.24 = (f32[8,16,1,256]{3,1,2,0:T(8,128)S(1)}, f32[8,16,1,256]{3,1,2,0:T(8,128)S(1)}, u32[]{:S(2)}, u32[]{:S(2)}) collective-permute-start(f32[8,16,1,256]{3,1,2,0:T(8,128)S(1)} %get-tuple-element.60), channel_id=1, source_target_pairs={{0,4},{4,8},{8,12},{12,16},{16,20},{20,24},{24,28},{28,32},{32,36}... | collective-permute-start | bytes 393224 | tf_op jit(solution)/shard_map/ppermute | solution.py:22
  515.9 10.4 %collective-permute-start.27 = (f32[8,16,1,256]{3,1,2,0:T(8,128)S(1)}, f32[8,16,1,256]{3,1,2,0:T(8,128)S(1)}, u32[]{:S(2)}, u32[]{:S(2)}) collective-permute-start(f32[8,16,1,256]{3,1,2,0:T(8,128)S(1)} %get-tuple-element.59), channel_id=1, source_target_pairs={{4,0},{8,4},{12,8},{16,12},{20,16},{24,20},{28,24},{32,28},{36,32}... | collective-permute-start | bytes 393224 | tf_op jit(solution)/shard_map/ppermute | solution.py:23
  517.2 10.6 %collective-permute-start.26 = (f32[8,16,1,256]{3,1,2,0:T(8,128)S(1)}, f32[8,16,1,256]{3,1,2,0:T(8,128)S(1)}, u32[]{:S(2)}, u32[]{:S(2)}) collective-permute-start(f32[8,16,1,256]{3,1,2,0:T(8,128)S(1)} %get-tuple-element.58), channel_id=1, source_target_pairs={{0,4},{4,8},{8,12},{12,16},{16,20},{20,24},{24,28},{28,32},{32,36}... | collective-permute-start | bytes 393224 | tf_op jit(solution)/shard_map/ppermute | solution.py:22
  529.0 9.8 %collective-permute-start.29 = (f32[8,16,1,256]{3,1,2,0:T(8,128)S(1)}, f32[8,16,1,256]{3,1,2,0:T(8,128)S(1)}, u32[]{:S(2)}, u32[]{:S(2)}) collective-permute-start(f32[8,16,1,256]{3,1,2,0:T(8,128)S(1)} %get-tuple-element.57), channel_id=1, source_target_pairs={{4,0},{8,4},{12,8},{16,12},{20,16},{24,20},{28,24},{32,28},{36,32}... | collective-permute-start | bytes 393224 | tf_op jit(solution)/shard_map/ppermute | solution.py:23
  530.3 10.0 %collective-permute-start.28 = (f32[8,16,1,256]{3,1,2,0:T(8,128)S(1)}, f32[8,16,1,256]{3,1,2,0:T(8,128)S(1)}, u32[]{:S(2)}, u32[]{:S(2)}) collective-permute-start(f32[8,16,1,256]{3,1,2,0:T(8,128)S(1)} %get-tuple-element.56), channel_id=1, source_target_pairs={{0,4},{4,8},{8,12},{12,16},{16,20},{20,24},{24,28},{28,32},{32,36}... | collective-permute-start | bytes 393224 | tf_op jit(solution)/shard_map/ppermute | solution.py:22
  541.6 9.5 %collective-permute-start.31 = (f32[8,16,1,256]{3,1,2,0:T(8,128)S(1)}, f32[8,16,1,256]{3,1,2,0:T(8,128)S(1)}, u32[]{:S(2)}, u32[]{:S(2)}) collective-permute-start(f32[8,16,1,256]{3,1,2,0:T(8,128)S(1)} %get-tuple-element.55), channel_id=1, source_target_pairs={{4,0},{8,4},{12,8},{16,12},{20,16},{24,20},{28,24},{32,28},{36,32}... | collective-permute-start | bytes 393224 | tf_op jit(solution)/shard_map/ppermute | solution.py:23
  542.9 10.0 %collective-permute-start.30 = (f32[8,16,1,256]{3,1,2,0:T(8,128)S(1)}, f32[8,16,1,256]{3,1,2,0:T(8,128)S(1)}, u32[]{:S(2)}, u32[]{:S(2)}) collective-permute-start(f32[8,16,1,256]{3,1,2,0:T(8,128)S(1)} %get-tuple-element.54), channel_id=1, source_target_pairs={{0,4},{4,8},{8,12},{12,16},{16,20},{20,24},{24,28},{28,32},{32,36}... | collective-permute-start | bytes 393224 | tf_op jit(solution)/shard_map/ppermute | solution.py:22
  554.2 12.3 %collective-permute-start.33 = (f32[8,16,1,256]{3,1,2,0:T(8,128)S(1)}, f32[8,16,1,256]{3,1,2,0:T(8,128)S(1)}, u32[]{:S(2)}, u32[]{:S(2)}) collective-permute-start(f32[8,16,1,256]{3,1,2,0:T(8,128)S(1)} %get-tuple-element.53), channel_id=1, source_target_pairs={{4,0},{8,4},{12,8},{16,12},{20,16},{24,20},{28,24},{32,28},{36,32}... | collective-permute-start | bytes 393224 | tf_op jit(solution)/shard_map/ppermute | solution.py:23
  555.5 12.5 %collective-permute-start.32 = (f32[8,16,1,256]{3,1,2,0:T(8,128)S(1)}, f32[8,16,1,256]{3,1,2,0:T(8,128)S(1)}, u32[]{:S(2)}, u32[]{:S(2)}) collective-permute-start(f32[8,16,1,256]{3,1,2,0:T(8,128)S(1)} %get-tuple-element.52), channel_id=1, source_target_pairs={{0,4},{4,8},{8,12},{12,16},{16,20},{20,24},{24,28},{28,32},{32,36}... | collective-permute-start | bytes 393224 | tf_op jit(solution)/shard_map/ppermute | solution.py:22
  (17 other events, 34.7 us)
Sparse Core Ops, SparseCore 0:
  242.8 83.8 all-reduce.2
  570.1 81.6 all-reduce.4
where the time goes:
time: 670 us; the launch traced here: 661 us
  other arithmetic  206 us (31%)
  waiting for transfers between devices  202 us (30%)
  starting transfers between devices  148 us (22%)
  local copies, waits for them, and re-layouts  88.7 us (13%)
  between operations  15.8 us (2%)
    psum x2, waiting for transfers between devices, reduced(): return lax.psum(term, 'mem') * scale  164 us
    scatter-add x8, other arithmetic, adjoint_obs(): flat = flat.at[:, cells[c]].add(weights[c] * contrib)  154 us
    ppermute x17, starting transfers between devices, padded(): before = lax.ppermute(last, axis, up)  111 us
    gather x8, local copies, waits for them, and re-layouts, on_device(): mixed = mixed + weights[c] * flat[:, cells[c]]  54.6 us
    ppermute x17, waiting for transfers between devices, padded(): before = lax.ppermute(last, axis, up)  22.4 us
    ppermute x17, starting transfers between devices, padded(): after = lax.ppermute(initial, axis, down)  22 us
    another operation x3, other arithmetic  18.2 us
    all_to_all x1, starting transfers between devices, on_device(): lax.all_to_all(buffer.reshape(width, tiles, slots), 'tile', split_axis=1,...  15.1 us
  transfers between devices with their start and end apart: 37, of which 33 were waited for; matrix products, arithmetic and copies ran while one was open for 1% of the time, Pallas kernels for 0%

commit v1 on v0

v1 whole, which is shorter than its diff:
```python
import functools
import math

import jax
import jax.numpy as jnp
from jax import lax
from jax.experimental import pallas as pl
from jax.experimental.pallas import tpu as pltpu
from jax.sharding import PartitionSpec as P

MESH = pl.DeviceIdType.MESH
BF = jnp.bfloat16
F32 = jnp.float32
DIFFUSIVITIES = (0.06, 0.1, 0.15, 0.22)
STEP = 0.5
MOST = 48
FEATURES = 32
HALO = 4
LANES = 128

(A2A, KAP_U, KAP_D, PERT_U, PERT_D, RS0, AG0, HU0, HD0, RSU, RUU, RUD, AGU, RS1, AG1, HU1, HD1,
 RSV, RVU, RVD, N_SEM) = range(21)


def nt(a, b):
    return lax.dot_general(a, b, (((1,), (1,)), ((), ())), preferred_element_type=F32)


def nn(a, b):
    return jnp.dot(a, b, preferred_element_type=F32)


def split2(x):
    hi = x.astype(BF).astype(F32)
    return hi, x - hi


def kernel(
    tiles, groups, members,
    pert_ref, classes_ref, target_ref, cells_ref, interp_ref, jac_ref, innov_ref, inv_ref,
    control_ref, incr_ref,
    perm, pay, val, out_buf, in_buf, feat, onehot, a_hi, a_lo,
    pert, stage, kap_rows, kap, cen, ikap,
    s0, s1, rs0, rs1, x0, x1, up, rsu, ruu, rud, u, vp, rsv, rvu, rvd, flat,
    ssem, rsem, lsem,
):
    t = lax.axis_index("tile")
    j = lax.axis_index("mem")
    north, south = lax.rem(t + tiles - 1, tiles), lax.rem(t + 1, tiles)
    slots = MOST // groups
    levels = 16
    scale = 1.0 / math.sqrt(members * groups - 1)
    obs = pay.shape[1]

    def peer(d):
        return lax.rem(j + d, groups)

    def band(d):
        return lax.rem(t + d, tiles)

    def send(src, dst, k, tile, mem):
        pltpu.make_async_remote_copy(
            src_ref=src, dst_ref=dst, send_sem=ssem.at[k], recv_sem=rsem.at[k],
            device_id={"tile": tile, "mem": mem}, device_id_type=MESH,
        ).start()

    def arrived(like, k):
        pltpu.make_async_copy(like, like, rsem.at[k]).wait()

    def sent(like, k):
        pltpu.make_async_copy(like, like, ssem.at[k]).wait()

    barrier = pltpu.get_barrier_semaphore()

    def greet(tile, mem):
        pl.semaphore_signal(
            barrier, inc=1, device_id={"tile": tile, "mem": mem}, device_id_type=MESH
        )

    def greet_band(d, carry):
        greet(band(d), j)
        return carry

    lax.fori_loop(1, tiles, greet_band, 0)
    for d in range(1, groups):
        greet(t, peer(d))
        greet(north, peer(d))
        greet(south, peer(d))

    row_id = lax.broadcasted_iota(jnp.int32, (256, 256), 0)
    col_id = lax.broadcasted_iota(jnp.int32, (256, 256), 1)
    perm[0] = jnp.where(col_id == (row_id & 1) * 128 + (row_id >> 1), 1.0, 0.0).astype(BF)
    perm[1] = jnp.where(row_id == (col_id & 1) * 128 + (col_id >> 1), 1.0, 0.0).astype(BF)

    target = target_ref[...]
    bands = lax.broadcasted_iota(jnp.int32, (tiles, obs), 0)
    member_of = jnp.where(target == bands, 1.0, 0.0)
    member_bf = member_of.astype(BF)
    before = jnp.where(row_id < col_id, 1.0, 0.0).astype(BF)
    base = jnp.zeros((tiles, 1), F32)
    ranks = []
    for b in range(obs // 256):
        part = slice(b * 256, (b + 1) * 256)
        count = nn(member_bf[:, part], before) + base
        ranks.append(jnp.sum(member_of[:, part] * count, axis=0, keepdims=True))
        base = base + jnp.sum(member_of[:, part], axis=1, keepdims=True)
    rank = jnp.concatenate(ranks, axis=1).astype(jnp.int32) - j * slots

    pay[0:16, :] = jac_ref[...]
    pay[16:24, :] = jnp.concatenate([cells_ref[...].astype(F32), interp_ref[...]], axis=0)
    pay[24:32, :] = jnp.concatenate(
        [innov_ref[...], inv_ref[...], jnp.zeros((6, obs), F32)], axis=0
    )
    whole = pay[...]
    high = whole.astype(BF).astype(F32)
    rest = whole - high
    middle = rest.astype(BF).astype(F32)
    low = rest - middle
    for q in range(slots):
        mine = rank == q
        for k, piece in enumerate((high, middle, low)):
            val[k, q * FEATURES : (q + 1) * FEATURES, :] = jnp.where(mine, piece, 0.0).astype(BF)
    packed = nt(member_bf, val[0]) + nt(member_bf, val[1]) + nt(member_bf, val[2])
    out_buf[:, 0, :] = packed

    def arrange(m, carry):
        block = pert_ref[m].astype(F32).reshape(levels * 8, 256).astype(BF)
        moved = nn(block, perm[0])
        stage[0] = moved[:, :LANES]
        stage[1] = moved[:, LANES:]
        for r in range(8):
            for lh in range(2):
                at = pl.ds(pl.multiple_of(m * levels + lh * 8, 8), 8)
                for h in range(2):
                    pert[HALO + r, h, at, :] = stage[h, pl.ds(lh * 64 + r, 8, stride=8), :]
        return carry

    lax.fori_loop(0, members, arrange, 0)

    classes = nn(classes_ref[...].astype(F32).astype(BF), perm[0])
    kappa = jnp.zeros(classes.shape, F32)
    for position, coefficient in enumerate(DIFFUSIVITIES):
        kappa = kappa + jnp.where(classes == float(position), coefficient, 0.0)
    kap_rows[1] = kappa

    pl.semaphore_wait(barrier, tiles - 1 + 3 * (groups - 1))

    def send_band(d, carry):
        send(out_buf.at[band(d)], in_buf.at[t], A2A, band(d), j)
        return carry

    lax.fori_loop(1, tiles, send_band, 0)
    own = pltpu.make_async_copy(out_buf.at[t], in_buf.at[t], lsem.at[0])
    own.start()
    send(kap_rows.at[1], kap_rows.at[0], KAP_U, south, j)
    send(kap_rows.at[1], kap_rows.at[2], KAP_D, north, j)
    send(pert.at[pl.ds(8, 4)], pert.at[pl.ds(0, 4)], PERT_U, south, j)
    send(pert.at[pl.ds(4, 4)], pert.at[pl.ds(12, 4)], PERT_D, north, j)

    arrived(kap_rows.at[0], KAP_U)
    arrived(kap_rows.at[2], KAP_D)
    for r in range(16):
        block, row = divmod(r + 4, 8)
        line = kap_rows[block, row : row + 1, :]
        if r < 4:
            line = jnp.where(t == 0, 0.0, line)
        if r >= 12:
            line = jnp.where(t == tiles - 1, 0.0, line)
        for h in range(2):
            wide = jnp.broadcast_to(line[:, h * LANES : (h + 1) * LANES], (8, LANES))
            kap[r, h] = wide
            cen[r, h] = 1.0 - 4.0 * wide
            if 4 <= r < 12:
                ikap[r - 4, h] = 1.0 / wide

    own.wait()
    arrived(in_buf.at[pl.ds(0, tiles - 1)], A2A)

    parts = [in_buf[:, 0, g * LANES : (g + 1) * LANES] for g in range(3)]
    pair = jnp.concatenate(parts[:2], axis=0).T
    last = jnp.concatenate([parts[2], parts[2]], axis=0).T
    for b in range(4):
        feat[b] = pair[b * FEATURES : (b + 1) * FEATURES, :]
    lane = lax.broadcasted_iota(jnp.int32, (FEATURES, LANES), 1)
    for b in range(2):
        one = last[2 * b * FEATURES : (2 * b + 1) * FEATURES, :]
        two = last[(2 * b + 1) * FEATURES : (2 * b + 2) * FEATURES, :]
        feat[4 + b] = jnp.where(lane < 64, one, two)
    blocks = 6

    def place(b, c):
        cell = feat[b, 16 + c : 17 + c, :].astype(jnp.int32)
        code = (cell & 1) * 8 + (cell >> 8)
        low = (cell & 255) >> 1
        return code, low

    def hits(code):
        return lax.broadcasted_iota(jnp.int32, (16, 8, LANES), 0) == code.reshape(1, 1, LANES)

    def build(b, carry):
        for c in range(4):
            low = place(b, c)[1]
            spot = lax.broadcasted_iota(jnp.int32, (LANES, LANES), 0) == low
            onehot[b, :, c * LANES : (c + 1) * LANES] = jnp.where(spot, 1.0, 0.0).astype(BF)
        return carry

    lax.fori_loop(0, blocks, build, 0)

    def adjoint_obs(b, z, total):
        jac = feat[b, 0:16, :]
        for c in range(4):
            code = place(b, c)[0]
            value = jac * (feat[b, 20 + c : 21 + c, :] * z)
            mask = hits(code)[None]
            for piece, where_to in zip(split2(value), (a_hi, a_lo)):
                wide = jnp.where(mask, piece.reshape(2, 1, 8, LANES), 0.0)
                where_to[:, c * LANES : (c + 1) * LANES] = wide.reshape(256, LANES).astype(BF)
        new = nt(a_hi[...], onehot[b]) + nt(a_lo[...], onehot[b])
        total[...] += new.reshape(4, 8, 8, LANES)

    def first(b, carry):
        z = -(feat[b, 25:26, :] * feat[b, 24:25, :])
        adjoint_obs(b, z, s0)
        return carry

    s0[...] = jnp.zeros(s0.shape, F32)
    lax.fori_loop(0, blocks, first, 0)

    def scatter(source, into, k):
        for d in range(1, groups):
            send(source.at[peer(d)], into.at[d - 1], k, t, peer(d))

    def spread(x, k, k_up, k_down):
        for d in range(1, groups):
            here = x.at[j, pl.ds(HALO, 8)]
            send(here, here, k, t, peer(d))
        for d in range(groups):
            send(x.at[j, pl.ds(8, 4)], x.at[j, pl.ds(0, 4)], k_up, south, peer(d))
            send(x.at[j, pl.ds(4, 4)], x.at[j, pl.ds(12, 4)], k_down, north, peer(d))
        arrived(x.at[pl.ds(0, groups - 1), pl.ds(HALO, 8)], k)
        arrived(x.at[:, pl.ds(0, 4)], k_up)
        arrived(x.at[:, pl.ds(12, 4)], k_down)

    scatter(s0, rs0, RS0)
    arrived(rs0, RS0)
    x0[j, pl.ds(HALO, 8)] = s0[j] + rs0[0] + rs0[1] + rs0[2]
    spread(x0, AG0, HU0, HD0)
    arrived(pert.at[pl.ds(0, 4)], PERT_U)
    arrived(pert.at[pl.ds(12, 4)], PERT_D)

    def sweep(f, lo, hi):
        even, odd = f
        n = hi - lo
        e, o = even[1 : 1 + n], odd[1 : 1 + n]
        ring_e = even[:n] + even[2:] + (o + pltpu.roll(o, 1, 2))
        ring_o = odd[:n] + odd[2:] + (e + pltpu.roll(e, LANES - 1, 2))
        return (
            cen[lo:hi, 0] * e + kap[lo:hi, 0] * ring_e,
            cen[lo:hi, 1] * o + kap[lo:hi, 1] * ring_o,
        )

    def local_pass(x, control_out):
        up[...] = jnp.zeros(up.shape, F32)

        def group(i, carry):
            lh, m = i // members, lax.rem(i, members)
            at = pl.ds(pl.multiple_of(m * levels + lh * 8, 8), 8)
            f = tuple(kap[:, h] * pert[:, h, at, :] * x[lh * 2 + h] for h in range(2))
            for k in range(4):
                f = sweep(f, k + 1, 15 - k)
            f = tuple(f[h] * ikap[:, h] for h in range(2))
            if control_out:
                for h in range(2):
                    for r in range(8):
                        stage_at = pl.ds(m * 128 + lh * 64 + r, 8, stride=8)
                        flat[h, stage_at, :] = f[h][r]
            zero = jnp.zeros((2, 8, LANES), F32)
            for k in range(4):
                f = sweep(
                    tuple(jnp.concatenate([zero, g, zero], axis=0) for g in f), 3 - k, 13 + k
                )
            for h in range(2):
                up[lh * 2 + h] += pert[:, h, at, :] * f[h]
            return carry

        lax.fori_loop(0, 2 * members, group, 0)

    def reduce(source, near, from_north, from_south, k, k_up, k_down):
        for d in range(1, groups):
            q = peer(d)
            send(source.at[q, pl.ds(HALO, 8)], near.at[d - 1], k, t, q)
        for d in range(groups):
            q = peer(d)
            send(source.at[q, pl.ds(12, 4)], from_north.at[j], k_up, south, q)
            send(source.at[q, pl.ds(0, 4)], from_south.at[j], k_down, north, q)
        arrived(near, k)
        arrived(from_north, k_up)
        arrived(from_south, k_down)
        total = source[j, pl.ds(HALO, 8)] + near[0] + near[1] + near[2]
        top = from_north[0] + from_north[1] + from_north[2] + from_north[3]
        bottom = from_south[0] + from_south[1] + from_south[2] + from_south[3]
        return total + jnp.concatenate([top, bottom], axis=0)

    local_pass(x0, False)
    u[j] = (-STEP * scale * scale) * reduce(up, rsu, ruu, rud, RSU, RUU, RUD)
    for d in range(1, groups):
        send(u.at[j], u.at[j], AGU, t, peer(d))
    arrived(u.at[pl.ds(0, groups - 1)], AGU)

    state_hi, state_lo = (g.astype(BF) for g in split2(u[...].reshape(256, LANES)))

    def second(b, carry):
        state_h, state_l = carry
        mixed = nn(state_h, onehot[b]) + nn(state_l, onehot[b])
        jac = feat[b, 0:16, :].reshape(2, 8, LANES)
        total = jnp.zeros((2, 8, LANES), F32)
        for c in range(4):
            mask = hits(place(b, c)[0])[None]
            part = mixed[:, c * LANES : (c + 1) * LANES].reshape(2, 16, 8, LANES)
            picked = jnp.sum(jnp.where(mask, part, 0.0), axis=1)
            total = total + feat[b, 20 + c : 21 + c, :].reshape(1, 1, LANES) * picked
        y = jnp.sum((jac * total).reshape(16, LANES), axis=0, keepdims=True)
        z = feat[b, 25:26, :] * (y - feat[b, 24:25, :])
        adjoint_obs(b, z, s1)
        return carry

    s1[...] = jnp.zeros(s1.shape, F32)
    lax.fori_loop(0, blocks, second, (state_hi, state_lo))

    scatter(s1, rs1, RS1)
    arrived(rs1, RS1)
    x1[j, pl.ds(HALO, 8)] = (-scale * STEP) * (
        STEP * x0[j, pl.ds(HALO, 8)] + s1[j] + rs1[0] + rs1[1] + rs1[2]
    )
    spread(x1, AG1, HU1, HD1)
    sent(rsu, RSU)
    sent(ruu, RUU)
    sent(rud, RUD)
    local_pass(x1, True)

    sub = lax.broadcasted_iota(jnp.int32, (16, 8, LANES), 1)
    for lh in range(2):
        even, odd = up[lh * 2], up[lh * 2 + 1]
        vp[lh * 2] = jnp.where(sub < 4, even, pltpu.roll(odd, 4, 1))
        vp[lh * 2 + 1] = jnp.where(sub < 4, pltpu.roll(even, 4, 1), odd)

    def unmix(m, carry):
        rows = pl.ds(pl.multiple_of(m * 128, 128), 128)
        wide = jnp.concatenate([flat[0, rows, :], flat[1, rows, :]], axis=1)
        hi, lo = split2(wide)
        back = nn(hi.astype(BF), perm[1]) + nn(lo.astype(BF), perm[1])
        control_ref[m] = back.reshape(levels, 8, 256)
        return carry

    lax.fori_loop(0, members, unmix, 0)

    final = scale * reduce(vp, rsv, rvu, rvd, RSV, RVU, RVD)
    wide = jnp.concatenate(
        [final.reshape(64, LANES), pltpu.roll(final, 4, 1).reshape(64, LANES)], axis=1
    )
    hi, lo = split2(wide)
    back = nn(hi.astype(BF), perm[1]) + nn(lo.astype(BF), perm[1])
    for h in range(2):
        stage[h, 0:64, :] = back[:, h * LANES : (h + 1) * LANES]
        for level in range(4):
            incr_ref[level, :, h * LANES : (h + 1) * LANES] = stage[h, pl.ds(level, 8, stride=8), :]

    sent(in_buf.at[pl.ds(0, tiles - 1)], A2A)
    sent(kap_rows.at[0], KAP_U)
    sent(kap_rows.at[2], KAP_D)
    sent(pert.at[pl.ds(0, 4)], PERT_U)
    sent(pert.at[pl.ds(12, 4)], PERT_D)
    for k in (RS0, AG0, AGU, RS1, AG1, RSV):
        sent(rs0, k)
    for k in (HU0, HD0, HU1, HD1, RVU, RVD):
        sent(ruu, k)


def on_device(tiles, groups, perturbations, classes, target, cells, interp, jac, innov, inverse):
    members, levels, rows, cols = perturbations.shape
    obs = target.shape[0]
    vm = pl.BlockSpec(memory_space=pltpu.VMEM)
    quarter = (groups, 8, 8, LANES)
    window = (groups, 16, 8, LANES)
    near = (groups - 1, 8, 8, LANES)
    halo = (groups, 4, 8, LANES)
    scratch = [
        ((2, 256, 256), BF),
        ((FEATURES, obs), F32),
        ((3, FEATURES * (MOST // groups), obs), BF),
        ((tiles, 1, FEATURES * (MOST // groups)), F32),
        ((tiles, 1, FEATURES * (MOST // groups)), F32),
        ((6, FEATURES, LANES), F32),
        ((6, LANES, 4 * LANES), BF),
        ((256, 4 * LANES), BF),
        ((256, 4 * LANES), BF),
        ((16, 2, members * levels, LANES), F32),
        ((2, LANES, LANES), F32),
        ((3, 8, 256), F32),
        ((16, 2, 8, LANES), F32),
        ((16, 2, 8, LANES), F32),
        ((8, 2, 8, LANES), F32),
        (quarter, F32), (quarter, F32),
        (near, F32), (near, F32),
        (window, F32), (window, F32),
        (window, F32),
        (near, F32), (halo, F32), (halo, F32),
        (quarter, F32),
        (window, F32),
        (near, F32), (halo, F32), (halo, F32),
        ((2, members * levels * rows, LANES), F32),
    ]
    return pl.pallas_call(
        functools.partial(kernel, tiles, groups, members),
        out_shape=(
            jax.ShapeDtypeStruct((members, levels, rows, cols), F32),
            jax.ShapeDtypeStruct((levels // groups, rows, cols), F32),
        ),
        in_specs=[vm] * 8,
        out_specs=(vm, vm),
        scratch_shapes=[pltpu.VMEM(shape, dtype) for shape, dtype in scratch]
        + [
            pltpu.SemaphoreType.DMA((N_SEM,)),
            pltpu.SemaphoreType.DMA((N_SEM,)),
            pltpu.SemaphoreType.DMA((1,)),
        ],
        compiler_params=pltpu.CompilerParams(
            collective_id=0, has_side_effects=True, vmem_limit_bytes=40 * 1024 * 1024
        ),
        name="assimilate",
    )(
        perturbations, classes, target.reshape(1, obs), cells, interp, jac,
        innov.reshape(1, obs), inverse.reshape(1, obs),
    )


def solution(mesh):
    in_specs = (
        P("mem", None, "tile", None),
        P("tile", None),
        P("tile", None),
        P(None, "tile"),
        P(None, "tile"),
        P(None, "tile"),
        P("tile"),
        P("tile"),
    )
    out_specs = (P("mem", None, "tile", None), P("mem", "tile", None))
    return jax.shard_map(
        functools.partial(on_device, mesh.shape["tile"], mesh.shape["mem"]),
        mesh=mesh, in_specs=in_specs, out_specs=out_specs, check_vma=False,
    )
```

time: 670 us -> 119 us (0.18); the launches traced: 661 us -> 118 us
  other arithmetic: 206 us -> 0 us
  waiting for transfers between devices: 202 us -> 0 us
  starting transfers between devices: 148 us -> 0 us
  Pallas kernels: 0 us -> 110 us
  local copies, waits for them, and re-layouts: 88.7 us -> 7.65 us
  between operations: 15.8 us -> 0.66 us
    psum x2 -> x0, waiting for transfers between devices: 164 us -> none  [reduced(): return lax.psum(term, 'mem') * scale]
    scatter-add x8 -> x0, other arithmetic: 154 us -> none  [adjoint_obs(): flat = flat.at[:, cells[c]].add(weights[c] * contrib)]
    ppermute x34 -> x0, starting transfers between devices: 133 us -> none  [the longest x17 111 us: padded(): before = lax.ppermute(last, axis, up)]
    pallas_call x0 -> x1, Pallas kernels: none -> 110 us  [on_device(): pl.pallas_call(functools.partial(kernel, tiles, groups, members), out_sha...]
    gather x8 -> x0, local copies, waits for them, and re-layouts: 54.6 us -> none  [on_device(): mixed = mixed + weights[c] * flat[:, cells[c]]]
    ppermute x34 -> x0, waiting for transfers between devices: 29.7 us -> none  [the longest x17 22.4 us: padded(): before = lax.ppermute(last, axis, up)]
    mul x46 -> x0, other arithmetic: 25.7 us -> none  [the longest x12 11.5 us: sweeps(): grid = grid * row_mask(rows, depth - first_index - 1)[:, None]]
    another operation x3 -> x0, other arithmetic: 18.2 us -> none
  transfers between devices with their start and end apart: 37 -> 0, of which waited for: 33 -> 0; matrix products, arithmetic and copies ran while one was open for 1% -> 0% of each run, Pallas kernels for 0% -> 0%
where the time goes in v1:
time: 119 us; the launch traced here: 118 us
  Pallas kernels  110 us (92%)
  local copies, waits for them, and re-layouts  7.65 us (6%)
    pallas_call x1, Pallas kernels, on_device(): pl.pallas_call(functools.partial(kernel, tiles, groups, members), out_sha...  110 us
    unnamed x18, local copies, waits for them, and re-layouts  7.65 us

profile of v1, /device:TPU:1, one launch (start us, length us, event | category | flops | bytes accessed | tf_op | source)
XLA Modules:
  0.0 118.4 jit_solution(200085810545515893)
XLA Ops:
  0.6 0.0 copy-start.5
  0.6 0.7 copy-done.5
  1.3 0.0 copy-start
  1.3 1.0 copy-done
  2.4 0.0 copy-start.1
  2.4 0.8 copy-done.1
  3.2 0.0 copy-start.2
  3.2 0.7 copy-done.2
  3.9 0.0 copy-start.3
  3.9 0.7 copy-done.3
  4.6 0.0 copy-start.4
  4.6 0.7 copy-done.4
  5.3 0.0 copy-start.6
  5.3 0.7 copy-done.6
  6.0 0.0 copy-start.7
  6.0 0.7 copy-done.7
  6.7 110.1 %assimilate.1 = (f32[8,16,8,256]{3,2,1,0:T(8,128)S(1)}, f32[4,8,256]{2,1,0:T(8,128)S(1)}) custom-call(bf16[8,16,8,256]{3,2,1,0:T(8,128)(2,1)S(1)} %copy-done, s32[8,256]{1,0:T(8,128)S(1)} %copy-done.4, s32[1,1024]{1,0:T(1,128)S(1)} %bitcast.3, s32[4,1024]{1,0:T(4,128)S(1)} %copy-done.2, f32[4,1024]{1,0:T(4,128)S(1)} %copy-done.3, f32[16,1024]{1,0:T(8,128)S(1)} %copy-done.1, ...), custom_call_target="tpu_custom_call" | custom-call | tf_op jit(solution)/shard_map/assimilate/pallas_call | solution.py:413
  116.8 1.0 copy.12
  117.8 0.6 copy.13
Async XLA Ops:
  0.6 0.7 copy-start.5
  1.3 1.0 copy-start
  2.4 0.8 copy-start.1
  3.2 0.7 copy-start.2
  3.9 0.7 copy-start.3
  4.6 0.7 copy-start.4
  5.3 0.7 copy-start.6
  6.0 0.7 copy-start.7

commit v2 on v1

--- a/solution.py
+++ b/solution.py
@@ -37,10 +37,11 @@
 
 def kernel(
     tiles, groups, members,
+    pert_hbm, classes_hbm, target_hbm, cells_hbm, interp_hbm, jac_hbm, innov_hbm, inv_hbm,
+    control_ref, incr_ref,
     pert_ref, classes_ref, target_ref, cells_ref, interp_ref, jac_ref, innov_ref, inv_ref,
-    control_ref, incr_ref,
     perm, pay, val, out_buf, in_buf, feat, onehot, a_hi, a_lo,
-    pert, stage, kap_rows, kap, cen, ikap,
+    pert, stage, kap_rows, kap, ikap,
     s0, s1, rs0, rs1, x0, x1, up, rsu, ruu, rud, u, vp, rsv, rvu, rvd, flat,
     ssem, rsem, lsem,
 ):
@@ -70,6 +71,17 @@
     def sent(like, k):
         pltpu.make_async_copy(like, like, ssem.at[k]).wait()
 
+    fetches = [
+        pltpu.make_async_copy(source, into, lsem.at[1 + k])
+        for k, (source, into) in enumerate((
+            (target_hbm, target_ref), (cells_hbm, cells_ref), (interp_hbm, interp_ref),
+            (jac_hbm, jac_ref), (innov_hbm, innov_ref), (inv_hbm, inv_ref),
+            (pert_hbm, pert_ref), (classes_hbm, classes_ref),
+        ))
+    ]
+    for fetch in fetches:
+        fetch.start()
+
     barrier = pltpu.get_barrier_semaphore()
 
     def greet(tile, mem):
@@ -91,6 +103,9 @@
     col_id = lax.broadcasted_iota(jnp.int32, (256, 256), 1)
     perm[0] = jnp.where(col_id == (row_id & 1) * 128 + (row_id >> 1), 1.0, 0.0).astype(BF)
     perm[1] = jnp.where(row_id == (col_id & 1) * 128 + (col_id >> 1), 1.0, 0.0).astype(BF)
+
+    for fetch in fetches[:6]:
+        fetch.wait()
 
     target = target_ref[...]
     bands = lax.broadcasted_iota(jnp.int32, (tiles, obs), 0)
@@ -123,6 +138,9 @@
     packed = nt(member_bf, val[0]) + nt(member_bf, val[1]) + nt(member_bf, val[2])
     out_buf[:, 0, :] = packed
 
+    for fetch in fetches[6:]:
+        fetch.wait()
+
     def arrange(m, carry):
         block = pert_ref[m].astype(F32).reshape(levels * 8, 256).astype(BF)
         moved = nn(block, perm[0])
@@ -169,7 +187,6 @@
         for h in range(2):
             wide = jnp.broadcast_to(line[:, h * LANES : (h + 1) * LANES], (8, LANES))
             kap[r, h] = wide
-            cen[r, h] = 1.0 - 4.0 * wide
             if 4 <= r < 12:
                 ikap[r - 4, h] = 1.0 / wide
 
@@ -249,41 +266,65 @@
     arrived(pert.at[pl.ds(12, 4)], PERT_D)
 
     def sweep(f, lo, hi):
-        even, odd = f
-        n = hi - lo
-        e, o = even[1 : 1 + n], odd[1 : 1 + n]
-        ring_e = even[:n] + even[2:] + (o + pltpu.roll(o, 1, 2))
-        ring_o = odd[:n] + odd[2:] + (e + pltpu.roll(e, LANES - 1, 2))
-        return (
-            cen[lo:hi, 0] * e + kap[lo:hi, 0] * ring_e,
-            cen[lo:hi, 1] * o + kap[lo:hi, 1] * ring_o,
-        )
+        out = {}
+        for r in range(lo, hi):
+            here = f.get(r)
+            beside = [f[n] for n in (r - 1, r + 1) if n in f]
+            pair = []
+            for h in range(2):
+                terms = [row[h] for row in beside]
+                if here is not None:
+                    other = here[1 - h]
+                    terms.append(other + pltpu.roll(other, (1, LANES - 1)[h], 1))
+                beside_all = functools.reduce(jnp.add, terms)
+                if here is None:
+                    pair.append(kap[r, h] * beside_all)
+                else:
+                    pair.append(here[h] + kap[r, h] * (beside_all - 4.0 * here[h]))
+            out[r] = pair
+        return out
 
     def local_pass(x, control_out):
         up[...] = jnp.zeros(up.shape, F32)
+        together = 4
 
         def group(i, carry):
-            lh, m = i // members, lax.rem(i, members)
-            at = pl.ds(pl.multiple_of(m * levels + lh * 8, 8), 8)
-            f = tuple(kap[:, h] * pert[:, h, at, :] * x[lh * 2 + h] for h in range(2))
+            ids = []
+            for g in range(together):
+                lh, m = g % 2, i * (together // 2) + g // 2
+                ids.append((lh, m, pl.ds(pl.multiple_of(m * levels + lh * 8, 8), 8)))
+            fields = [
+                {
+                    r: [kap[r, h] * pert[r, h, at, :] * x[lh * 2 + h, r] for h in range(2)]
+                    for r in range(16)
+                }
+                for lh, m, at in ids
+            ]
             for k in range(4):
-                f = sweep(f, k + 1, 15 - k)
-            f = tuple(f[h] * ikap[:, h] for h in range(2))
+                fields = [sweep(f, k + 1, 15 - k) for f in fields]
+            fields = [
+                {r: [f[r][h] * ikap[r - HALO, h] for h in range(2)] for r in f} for f in fields
+            ]
             if control_out:
+                for f, (lh, m, at) in zip(fields, ids):
+                    for r in range(8):
+                        place_at = pl.ds(m * 128 + lh * 64 + r, 8, stride=8)
+                        for h in range(2):
+                            flat[h, place_at, :] = f[HALO + r][h]
+            for k in range(4):
+                fields = [sweep(f, 3 - k, 13 + k) for f in fields]
+            for r in range(16):
                 for h in range(2):
-                    for r in range(8):
-                        stage_at = pl.ds(m * 128 + lh * 64 + r, 8, stride=8)
-                        flat[h, stage_at, :] = f[h][r]
-            zero = jnp.zeros((2, 8, LANES), F32)
-            for k in range(4):
-                f = sweep(
-                    tuple(jnp.concatenate([zero, g, zero], axis=0) for g in f), 3 - k, 13 + k
-                )
-            for h in range(2):
-                up[lh * 2 + h] += pert[:, h, at, :] * f[h]
+                    for half in range(2):
+                        terms = [
+                            pert[r, h, at, :] * f[r][h]
+                            for f, (lh, m, at) in zip(fields, ids)
+                            if lh == half
+                        ]
+                        up[half * 2 + h, r] += functools.reduce(jnp.add, terms)
             return carry
 
-        lax.fori_loop(0, 2 * members, group, 0)
+        lax.fori_loop(0, 2 * members // together, group, 0)
 
     def reduce(source, near, from_north, from_south, k, k_up, k_down):
         for d in range(1, groups):
@@ -380,11 +421,20 @@
     members, levels, rows, cols = perturbations.shape
     obs = target.shape[0]
     vm = pl.BlockSpec(memory_space=pltpu.VMEM)
+    hbm = pl.BlockSpec(memory_space=pltpu.HBM)
     quarter = (groups, 8, 8, LANES)
     window = (groups, 16, 8, LANES)
     near = (groups - 1, 8, 8, LANES)
     halo = (groups, 4, 8, LANES)
     scratch = [
+        (perturbations.shape, perturbations.dtype),
+        (classes.shape, classes.dtype),
+        ((1, obs), target.dtype),
+        (cells.shape, cells.dtype),
+        (interp.shape, interp.dtype),
+        (jac.shape, jac.dtype),
+        ((1, obs), innov.dtype),
+        ((1, obs), inverse.dtype),
         ((2, 256, 256), BF),
         ((FEATURES, obs), F32),
         ((3, FEATURES * (MOST // groups), obs), BF),
@@ -397,7 +447,6 @@
         ((16, 2, members * levels, LANES), F32),
         ((2, LANES, LANES), F32),
         ((3, 8, 256), F32),
-        ((16, 2, 8, LANES), F32),
         ((16, 2, 8, LANES), F32),
         ((8, 2, 8, LANES), F32),
         (quarter, F32), (quarter, F32),
@@ -416,13 +465,13 @@
             jax.ShapeDtypeStruct((members, levels, rows, cols), F32),
             jax.ShapeDtypeStruct((levels // groups, rows, cols), F32),
         ),
-        in_specs=[vm] * 8,
+        in_specs=[hbm] * 8,
         out_specs=(vm, vm),
         scratch_shapes=[pltpu.VMEM(shape, dtype) for shape, dtype in scratch]
         + [
             pltpu.SemaphoreType.DMA((N_SEM,)),
             pltpu.SemaphoreType.DMA((N_SEM,)),
-            pltpu.SemaphoreType.DMA((1,)),
+            pltpu.SemaphoreType.DMA((9,)),
         ],
         compiler_params=pltpu.CompilerParams(
             collective_id=0, has_side_effects=True, vmem_limit_bytes=40 * 1024 * 1024

time: 119 us -> 104 us (0.87)
  Pallas kernels: 110 us -> 95.4 us
    pallas_call x1, Pallas kernels: 110 us -> 95.4 us  [on_device(): pl.pallas_call(functools.partial(kernel, tiles, groups, members), out_sha...]
where the time goes in v2:
time: 104 us
  Pallas kernels  95.4 us (92%)
  local copies, waits for them, and re-layouts  7.65 us (7%)
    pallas_call x1, Pallas kernels, on_device(): pl.pallas_call(functools.partial(kernel, tiles, groups, members), out_sha...  95.4 us
    unnamed x18, local copies, waits for them, and re-layouts  7.65 us

profile of v2, /device:TPU:1, one launch (start us, length us, event | category | flops | bytes accessed | tf_op | source)
XLA Modules:
  0.0 103.7 jit_solution(4368998365867176741)
XLA Ops:
  0.6 0.0 copy-start.5
  0.6 0.7 copy-done.5
  1.3 0.0 copy-start
  1.3 1.0 %copy-done = bf16[8,16,8,256]{3,2,1,0:T(8,128)(2,1)S(1)} copy-done((bf16[8,16,8,256]{3,2,1,0:T(8,128)(2,1)S(1)}, bf16[8,16,8,256]{3,2,1,0:T(8,128)(2,1)}, u32[]{:S(2)}) %copy-start) | copy-done | bytes 524312
  2.4 0.0 copy-start.1
  2.4 0.8 copy-done.1
  3.2 0.0 copy-start.2
  3.2 0.7 copy-done.2
  3.9 0.0 copy-start.3
  3.9 0.7 copy-done.3
  4.6 0.0 copy-start.4
  4.6 0.7 copy-done.4
  5.3 0.0 copy-start.6
  5.3 0.7 copy-done.6
  6.0 0.0 copy-start.7
  6.0 0.7 copy-done.7
  6.7 95.4 %assimilate.1 = (f32[8,16,8,256]{3,2,1,0:T(8,128)S(1)}, f32[4,8,256]{2,1,0:T(8,128)S(1)}) custom-call(bf16[8,16,8,256]{3,2,1,0:T(8,128)(2,1)S(1)} %copy-done, s32[8,256]{1,0:T(8,128)S(1)} %copy-done.4, s32[1,1024]{1,0:T(1,128)S(1)} %bitcast.3, s32[4,1024]{1,0:T(4,128)S(1)} %copy-done.2, f32[4,1024]{1,0:T(4,128)S(1)} %copy-done.3, f32[16,1024]{1,0:T(8,128)S(1)} %copy-done.1, ...), custom_call_target="tpu_custom_call" | custom-call | tf_op jit(solution)/shard_map/assimilate/pallas_call | solution.py:462
  102.1 1.0 copy.12
  103.0 0.6 copy.13
Async XLA Ops:
  0.6 0.7 copy-start.5
  1.3 1.0 %copy-start = (bf16[8,16,8,256]{3,2,1,0:T(8,128)(2,1)S(1)}, bf16[8,16,8,256]{3,2,1,0:T(8,128)(2,1)}, u32[]{:S(2)}) copy-start(bf16[8,16,8,256]{3,2,1,0:T(8,128)(2,1)} %pert_hbm.1) | copy-start | bytes 1572868
  2.4 0.8 copy-start.1
  3.2 0.7 copy-start.2
  3.9 0.7 copy-start.3
  4.6 0.7 copy-start.4
  5.3 0.7 copy-start.6
  6.0 0.7 copy-start.7
